TPU v7x, 256 devices: a whole 4x4x8 slice. The times are simulated.
256 devices in a mesh: outer: 4 (over x_hi, core), dp: 64 (over y, x_lo, z).
Axes of the slice: x: 4 (x_hi: 2, x_lo: 2; x = x_hi * 2 + x_lo), y: 4, z: 8, core: 2. Of those that a mesh axis runs over, the one named last changes fastest.
Arguments:
- videos: bfloat16 [4096, 1024], P(('outer', 'dp'))
- captions: bfloat16 [131072, 1024], P(('outer', 'dp'))
- caption_owner: int32 [131072], P(('outer', 'dp')), may hold values from 0 to 4095, as said below
- log_temp: float32 [1], replicated, may hold values from 2 to 2.8
- bias: float32 [1], replicated, may hold values from -6 to -3
Outputs:
- video_grad: float32 [4096, 1024], P(('outer', 'dp'))
- caption_grad: float32 [131072, 1024], P(('outer', 'dp'))
- scalars: float32 [3], replicated
Inputs may be any that keep to these rules, and one draw needn't show every extreme that they name: Captions stand in video order: caption_owner never falls, every video owns between 24 and 40 consecutive captions, videos 2k and 2k+1 together own exactly 64 captions, and some video owns exactly 40.
All inputs are finite; a program needn't handle non-finite values.
Results may differ from a plain program's by a relative error of at most 0.0023.
Values may be sent and summed in bfloat16 or wider, within the bound.
A program may use at most 128 MiB of HBM per device.

v0:
```python
import jax
import jax.numpy as jnp
from jax import lax
from jax.sharding import PartitionSpec as P


def from_behind(value, axis, steps):
    count = lax.axis_size(axis)
    pairs = [(source, (source + steps) % count) for source in range(count)]
    return lax.ppermute(value, axis, pairs)


def unit_rows(values):
    widened = values.astype(jnp.float32)
    row_scale = lax.rsqrt(jnp.sum(widened * widened, axis=1, keepdims=True) + 1e-06)
    return (row_scale, widened * row_scale)


def back_rows(row_scale, unit_vals, incoming):
    return row_scale * (incoming - unit_vals * jnp.sum(unit_vals * incoming, axis=1, keepdims=True))


def pair_block(video_rows, first_video, caption_low, owners, temper, bias_value):
    video_ids = first_video + jnp.arange(video_rows.shape[0], dtype=jnp.int32)
    logits = (
        temper
        * lax.dot_general(
            video_rows, caption_low, (((1,), (1,)), ((), ())), preferred_element_type=jnp.float32
        )
        + bias_value
    )
    signs = jnp.where(owners[None, :] == video_ids[:, None], 1.0, -1.0)
    pair_grad = -signs * jax.nn.sigmoid(-signs * logits)
    pair_low = pair_grad.astype(jnp.bfloat16)
    video_part = temper * jnp.dot(pair_low, caption_low, preferred_element_type=jnp.float32)
    caption_part = lax.dot_general(
        pair_low, video_rows, (((0,), (0,)), ((), ())), preferred_element_type=jnp.float32
    )
    block_sums = jnp.stack(
        [
            jnp.sum(-jax.nn.log_sigmoid(signs * logits)),
            jnp.sum(pair_grad * (logits - bias_value)),
            jnp.sum(pair_grad),
        ]
    )
    return (video_part, caption_part, block_sums)


def on_device(videos, captions, caption_owner, log_temp, bias):
    vid_dev = videos.shape[0]
    cap_dev = captions.shape[0]
    feature_width = videos.shape[1]
    outer_count = lax.axis_size("outer")
    group_count = lax.axis_size("dp")
    panel_rows = vid_dev * group_count
    all_rows = panel_rows * outer_count
    video_scale, video_unit = unit_rows(videos)
    video_low = video_unit.astype(jnp.bfloat16)
    caption_scale, caption_unit = unit_rows(captions)
    caption_low = caption_unit.astype(jnp.bfloat16)
    temper = jnp.exp(log_temp[0])
    bias_value = bias[0]
    cap_sum = jnp.zeros((cap_dev, feature_width), jnp.float32)
    totals = jnp.zeros((3,), jnp.float32)
    outer_at = lax.axis_index("outer")
    panel_low = lax.all_gather(video_low, "dp", axis=0, tiled=True)
    return_slots = jnp.zeros((outer_count, vid_dev, feature_width), jnp.float32)
    for travel in range(outer_count):
        if travel > 0:
            panel_low = from_behind(panel_low, "outer", 1)
        source_group = (outer_at - travel) % outer_count
        video_part, caption_part, block_sums = pair_block(
            panel_low, source_group * panel_rows, caption_low, caption_owner, temper, bias_value
        )
        cap_sum = cap_sum + caption_part
        totals = totals + block_sums
        own_share = lax.psum_scatter(video_part, "dp", scatter_dimension=0, tiled=True)
        return_slots = lax.dynamic_update_slice_in_dim(
            return_slots, own_share[None], source_group, 0
        )
    returned = lax.all_to_all(return_slots, "outer", split_axis=0, concat_axis=0, tiled=True)
    own_grad = jnp.sum(returned, axis=0)
    totals = lax.psum(totals, ("outer", "dp"))
    scalars = totals / (float(all_rows) * float(cap_dev * outer_count * group_count))
    video_grad = back_rows(video_scale, video_unit, own_grad)
    caption_grad = back_rows(caption_scale, caption_unit, temper * cap_sum)
    return (video_grad, caption_grad, scalars)


def solution(mesh):
    in_specs = (P(("outer", "dp"), None), P(("outer", "dp"), None), P(("outer", "dp")), P(), P())
    out_specs = (P(("outer", "dp"), None), P(("outer", "dp"), None), P())
    return jax.shard_map(
        on_device, mesh=mesh, in_specs=in_specs, out_specs=out_specs, check_vma=False
    )
```

profile of v0, /device:TPU:1, one launch (start us, length us, event | category | flops | bytes accessed | tf_op | source)
XLA Modules:
  0.0 1616.0 jit_solution(14338294308847977793)
XLA Ops:
  7.2 0.0 all-gather.2.cloned.1.call-start
  7.2 0.9 fusion.56
  8.1 1.5 fusion.52
  9.6 0.0 reduce-scatter.5.cloned.1.call-start
  11.0 1.5 fusion.14
  12.5 257.6 %all-gather.2.cloned.1.call-done = bf16[1024,1024]{1,0:T(8,128)(2,1)} async-done(((bf16[16,1024]{1,0:T(8,128)(2,1)}), bf16[1024,1024]{1,0:T(8,128)(2,1)}) %all-gather.2.cloned.1.call-update) | async-done | bytes 2097168 | tf_op jit(solution)/shard_map/all_gather | solution.py:66
  270.1 3.3 multiply_add_fusion.3
  273.4 3.7 convolution_multiply_fusion.3
  277.1 0.0 reduce-scatter.7.cloned.1.call-start
  277.2 1.5 copy-done.2
  278.7 46.9 %collective-permute-start = (bf16[1024,1024]{1,0:T(8,128)(2,1)S(1)}, bf16[1024,1024]{1,0:T(8,128)(2,1)}, u32[]{:S(2)}, u32[]{:S(2)}) collective-permute-start(bf16[1024,1024]{1,0:T(8,128)(2,1)S(1)} %copy-done.2), channel_id=1, source_target_pairs={{0,64},{64,128},{128,192},{192,0},{1,65},{65,129},{129,193},{193,1... | collective-permute-start | bytes 6291464 | tf_op jit(solution)/shard_map/ppermute | solution.py:10
  325.6 27.5 %collective-permute-done = bf16[1024,1024]{1,0:T(8,128)(2,1)} collective-permute-done((bf16[1024,1024]{1,0:T(8,128)(2,1)S(1)}, bf16[1024,1024]{1,0:T(8,128)(2,1)}, u32[]{:S(2)}, u32[]{:S(2)}) %collective-permute-start) | collective-permute-done | bytes 2097184 | tf_op jit(solution)/shard_map/ppermute | solution.py:10
  353.2 3.0 multiply_add_fusion.2
  356.1 1.4 copy-done.5
  357.5 3.7 convolution_multiply_fusion.2
  361.3 0.0 reduce-scatter.9.cloned.1.call-start
  361.3 4.2 collective-permute-start.1
  365.5 28.0 %collective-permute-done.1 = bf16[1024,1024]{1,0:T(8,128)(2,1)} collective-permute-done((bf16[1024,1024]{1,0:T(8,128)(2,1)}, bf16[1024,1024]{1,0:T(8,128)(2,1)}, u32[]{:S(2)}, u32[]{:S(2)}) %collective-permute-start.1) | collective-permute-done | bytes 2097184 | tf_op jit(solution)/shard_map/ppermute | solution.py:10
  393.5 3.0 multiply_add_fusion.1
  396.5 1.3 copy-done.7
  397.8 3.7 convolution_multiply_fusion.1
  401.6 0.0 reduce-scatter.11.cloned.1.call-start
  401.6 4.2 collective-permute-start.2
  405.9 27.5 %collective-permute-done.2 = bf16[1024,1024]{1,0:T(8,128)(2,1)} collective-permute-done((bf16[1024,1024]{1,0:T(8,128)(2,1)}, bf16[1024,1024]{1,0:T(8,128)(2,1)}, u32[]{:S(2)}, u32[]{:S(2)}) %collective-permute-start.2) | collective-permute-done | bytes 2097184 | tf_op jit(solution)/shard_map/ppermute | solution.py:10
  433.4 12.9 fusion.38
  446.3 1.3 copy-done.9
  447.6 3.7 convolution_multiply_fusion
  451.3 4.7 fusion.47
  456.0 4.8 fusion.44
  460.8 7.8 fusion.58
  468.6 4.5 fusion.41
  473.1 76.5 %psum.7 = f32[3]{0:T(128)S(1)} all-reduce(f32[3]{0:T(128)S(1)} %fusion.58), channel_id=1, replica_groups=mesh['outer'=4,'dp'=64] {'outer','dp'}, use_global_device_ids=true, to_apply=%region_21.22 | all-reduce | flops 3 | bytes 24 | tf_op jit(solution)/shard_map/psum | solution.py:83
  549.7 6.0 fusion.11
  555.7 1.7 fusion.13
  557.4 34.3 %reduce-scatter.5.cloned.1.call-done = f32[16,1024]{1,0:T(8,128)} async-done(((f32[1024,1024]{1,0:T(8,128)}), f32[16,1024]{1,0:T(8,128)}) %reduce-scatter.5.cloned.1.call-update) | async-done | bytes 65552 | tf_op jit(solution)/shard_map/reduce_scatter | solution.py:77
  591.7 0.7 broadcast_in_dim.41
  592.4 1.5 bitcast_dynamic-update-slice_fusion.3
  593.9 318.0 %reduce-scatter.7.cloned.1.call-done = f32[16,1024]{1,0:T(8,128)} async-done(((f32[1024,1024]{1,0:T(8,128)}), f32[16,1024]{1,0:T(8,128)}) %reduce-scatter.7.cloned.1.call-update) | async-done | bytes 65552 | tf_op jit(solution)/shard_map/reduce_scatter | solution.py:77
  911.9 1.5 bitcast_dynamic-update-slice_fusion.2
  913.4 315.3 %reduce-scatter.9.cloned.1.call-done = f32[16,1024]{1,0:T(8,128)} async-done(((f32[1024,1024]{1,0:T(8,128)}), f32[16,1024]{1,0:T(8,128)}) %reduce-scatter.9.cloned.1.call-update) | async-done | bytes 65552 | tf_op jit(solution)/shard_map/reduce_scatter | solution.py:77
  1228.7 1.5 bitcast_dynamic-update-slice_fusion.1
  1230.2 317.4 %reduce-scatter.11.cloned.1.call-done = f32[16,1024]{1,0:T(8,128)} async-done(((f32[1024,1024]{1,0:T(8,128)}), f32[16,1024]{1,0:T(8,128)}) %reduce-scatter.11.cloned.1.call-update) | async-done | bytes 65552 | tf_op jit(solution)/shard_map/reduce_scatter | solution.py:77
  1547.5 1.5 bitcast_dynamic-update-slice_fusion
  1549.0 52.8 %all-to-all-start = ((f32[4,16,1024]{2,1,0:T(8,128)}), f32[4,16,1024]{2,1,0:T(8,128)S(1)}, u32[]{:S(2)}, u32[]{:S(2)}) async-start(f32[4,16,1024]{2,1,0:T(8,128)} %bitcast_dynamic-update-slice_fusion), calls=%async_computation.4 | async-start | bytes 524288 | tf_op jit(solution)/shard_map/all_to_all | solution.py:81
  1601.8 0.5 broadcast_multiply_fusion
  1602.4 6.2 all-to-all-done
  1608.5 0.2 fusion.53
  1608.7 0.7 fusion.55
  (28 shorter events, 0.2 us)
Async XLA Ops:
  7.2 262.9 %all-gather.2.cloned.1.call-start = ((), (), s32[]{:S(2)}) async-start(), calls=%async_computation.5 | async-start | bytes 2129920 | tf_op jit(solution)/shard_map/all_gather | solution.py:66
  9.6 582.2 %reduce-scatter.5.cloned.1.call-start = ((), (), s32[]{:S(2)}) async-start(), calls=%async_computation.6 | async-start | bytes 4259840 | tf_op jit(solution)/shard_map/reduce_scatter | solution.py:77
  270.1 3.3 copy-start
  270.1 3.3 copy-start.3
  273.4 3.7 copy-start.4
  277.1 1.6 copy-start.2
  277.1 634.8 %reduce-scatter.7.cloned.1.call-start = ((), (), s32[]{:S(2)}) async-start(), calls=%async_computation.7 | async-start | bytes 4259840 | tf_op jit(solution)/shard_map/reduce_scatter | solution.py:77
  278.7 74.5 %collective-permute-start = (bf16[1024,1024]{1,0:T(8,128)(2,1)S(1)}, bf16[1024,1024]{1,0:T(8,128)(2,1)}, u32[]{:S(2)}, u32[]{:S(2)}) collective-permute-start(bf16[1024,1024]{1,0:T(8,128)(2,1)S(1)} %copy-done.2), channel_id=1, source_target_pairs={{0,64},{64,128},{128,192},{192,0},{1,65},{65,129},{129,193},{193,1... | collective-permute-start | bytes 6291464 | tf_op jit(solution)/shard_map/ppermute | solution.py:10
  356.1 1.4 copy-start.5
  361.3 867.4 %reduce-scatter.9.cloned.1.call-start = ((), (), s32[]{:S(2)}) async-start(), calls=%async_computation.8 | async-start | bytes 4259840 | tf_op jit(solution)/shard_map/reduce_scatter | solution.py:77
  361.3 32.2 %collective-permute-start.1 = (bf16[1024,1024]{1,0:T(8,128)(2,1)}, bf16[1024,1024]{1,0:T(8,128)(2,1)}, u32[]{:S(2)}, u32[]{:S(2)}) collective-permute-start(bf16[1024,1024]{1,0:T(8,128)(2,1)} %collective-permute-done), channel_id=1, source_target_pairs={{0,64},{64,128},{128,192},{192,0},{1,65},{65,129},{129,193},{193,1... | collective-permute-start | bytes 6291464 | tf_op jit(solution)/shard_map/ppermute | solution.py:10
  396.5 1.3 copy-start.7
  401.6 1146.0 %reduce-scatter.11.cloned.1.call-start = ((), (), s32[]{:S(2)}) async-start(), calls=%async_computation.9 | async-start | bytes 4259840 | tf_op jit(solution)/shard_map/reduce_scatter | solution.py:77
  401.6 31.7 %collective-permute-start.2 = (bf16[1024,1024]{1,0:T(8,128)(2,1)}, bf16[1024,1024]{1,0:T(8,128)(2,1)}, u32[]{:S(2)}, u32[]{:S(2)}) collective-permute-start(bf16[1024,1024]{1,0:T(8,128)(2,1)} %collective-permute-done.1), channel_id=1, source_target_pairs={{0,64},{64,128},{128,192},{192,0},{1,65},{65,129},{129,193},{193,1... | collective-permute-start | bytes 6291464 | tf_op jit(solution)/shard_map/ppermute | solution.py:10
  446.3 1.3 copy-start.9
  451.3 4.7 copy-start.6
  456.0 12.6 copy-start.8
  555.7 1052.8 %copy-start.1 = (bf16[16,1024]{1,0:T(8,128)(2,1)S(1)}, bf16[16,1024]{1,0:T(8,128)(2,1)}, u32[]{:S(2)}) copy-start(bf16[16,1024]{1,0:T(8,128)(2,1)} %param.5) | copy-start | bytes 98308
  1549.0 59.5 %all-to-all-start = ((f32[4,16,1024]{2,1,0:T(8,128)}), f32[4,16,1024]{2,1,0:T(8,128)S(1)}, u32[]{:S(2)}, u32[]{:S(2)}) async-start(f32[4,16,1024]{2,1,0:T(8,128)} %bitcast_dynamic-update-slice_fusion), calls=%async_computation.4 | async-start | bytes 524288 | tf_op jit(solution)/shard_map/all_to_all | solution.py:81
Sparse Core Ops, SparseCore 0:
  10.4 259.6 all-gather.1
  277.2 314.4 reduce-scatter.4
  594.4 317.4 reduce-scatter.6
  914.3 314.3 reduce-scatter.8
  1231.2 316.2 reduce-scatter.10
where the time goes:
time: 1620 us
  waiting for transfers between devices  1330 us (82%)
  starting transfers between devices  108 us (7%)
  blocking collectives  76.5 us (5%)
  matrix products  57.1 us (4%)
    reduce_scatter x4, waiting for transfers between devices, on_device(): lax.psum_scatter(video_part, 'dp', scatter_dimension=0, tiled=True)  985 us
    all_gather x1, waiting for transfers between devices, on_device(): panel_low = lax.all_gather(video_low, 'dp', axis=0, tiled=True)  258 us
    ppermute x3, waiting for transfers between devices, from_behind(): return lax.ppermute(value, axis, pairs)  83.1 us
    psum x1, blocking collectives, on_device(): totals = lax.psum(totals, ('outer', 'dp'))  76.5 us
    ppermute x3, starting transfers between devices, from_behind(): return lax.ppermute(value, axis, pairs)  55.3 us
    all_to_all x1, starting transfers between devices, on_device(): lax.all_to_all(return_slots, 'outer', split_axis=0, concat_axis=0, tiled=...  52.8 us
  transfers between devices with their start and end apart: 9, of which 9 were waited for; matrix products, arithmetic and copies ran while one was open for 4% of the time, Pallas kernels for 0%

commit v1 on v0

v1 whole, which is shorter than its diff:
```python
import jax
import jax.numpy as jnp
from jax import lax
from jax.experimental import pallas as pl
from jax.experimental.pallas import tpu as pltpu
from jax.sharding import PartitionSpec as P

MESH = pl.DeviceIdType.MESH
F32 = jnp.float32
BF16 = jnp.bfloat16
LOG2E = 1.4426950408889634
D = 1024
OWN = 16
CAP = 512
ALL = 4 * CAP
COPIES = 96


def device_at(x, y, z, core):
    return ((x // 2) * 2 + core, (y * 2 + x % 2) * 8 + z)


def kernel(
    videos, captions, owner, log_temp, bias,
    video_out, caption_out, scalar_out,
    G, C, V, PR, VA, VB, FA, FB,
    R1, RU, RM, TM, TP, RP, S2, TZ, RZ,
    TN1, RN1, TN2, RN2, TS, RS, CG, SC,
    send_sem, recv_sem,
):
    outer, inner = lax.axis_index("outer"), lax.axis_index("dp")
    x = (outer // 2) * 2 + (inner // 8) % 2
    y = inner // 16
    z = inner % 8
    core = outer % 2
    zh, zp = z // 2, z % 2

    def at(dx=0, dy=0, dz=0, other=False):
        return device_at(
            (x + dx + 4) % 4, (y + dy + 4) % 4, (z + dz + 8) % 8, 1 - core if other else core
        )

    started = []

    def send(src, dst, device):
        index = len(started)
        copy = pltpu.make_async_remote_copy(
            src_ref=src, dst_ref=dst, send_sem=send_sem.at[index], recv_sem=recv_sem.at[index],
            device_id=device, device_id_type=MESH,
        )
        copy.start()
        started.append(copy)
        return copy

    partners = [at(dx=i) for i in (1, 2, 3)] + [at(dy=i) for i in (1, 2, 3)]
    partners += [at(dz=i) for i in (1, 2, 4, 6, 7)] + [at(other=True)]
    barrier = pltpu.get_barrier_semaphore()
    for device in partners:
        pl.semaphore_signal(barrier, inc=1, device_id=device, device_id_type=MESH)

    temper = jnp.exp(jnp.full((1, 1), log_temp[0], F32))
    bias_value = bias[0]

    wide = videos[...].astype(F32)
    video_scale = lax.rsqrt(jnp.sum(wide * wide, axis=1, keepdims=True) + 1e-06)
    own_rows = pl.ds(pl.multiple_of(zh * OWN, OWN), OWN)
    G[x, y, own_rows, :] = (wide * video_scale).astype(BF16)

    pl.semaphore_wait(barrier, len(partners))

    mine = G.at[x, y, own_rows]
    along_z = [send(mine, mine, at(dz=2 * i)) for i in (1, 2, 3)]

    def low_captions(i, carry):
        rows = pl.ds(pl.multiple_of(i * 128, 128), 128)
        block = captions[rows, :].astype(F32)
        scale = lax.rsqrt(jnp.sum(block * block, axis=1, keepdims=True) + 1e-06)
        C[rows, :] = (block * scale).astype(BF16)
        return carry

    lax.fori_loop(0, CAP // 128, low_captions, 0)
    cap_up = send(C.at[0:256], C.at[1024:1280], at(dz=1))
    cap_down = send(C.at[256:512], C.at[1280:1536], at(dz=-1))
    cap_side = send(C.at[0:512], C.at[512:1024], at(other=True))

    for copy in along_z:
        copy.wait_recv()

    def unit_a(px, py, lo=0, hi=32):
        return G.at[(px + 4) % 4, (py + 4) % 4, lo:hi]

    def unit_b(px, py, lo=32, hi=64):
        return G.at[(px + 4) % 4, (py + 4) % 4, lo:hi]

    def same(unit, device):
        return send(unit, unit, device)

    ax_p, ax_m, by_p, by_m = {}, {}, {}, {}
    ax_p[0] = same(unit_a(x, y), at(dx=1))
    by_p[0] = same(unit_b(x, y), at(dy=1))
    ax_m[0] = same(unit_a(x, y), at(dx=-1))
    by_m[0] = same(unit_b(x, y), at(dy=-1))
    a_y, b_x = {}, {}
    for i in (1, 3, 2):
        a_y[i] = same(unit_a(x, y), at(dy=i))
        b_x[i] = same(unit_b(x, y), at(dx=i))
    for i in (1, 3, 2):
        a_y[i].wait_recv()
        ax_p[i] = same(unit_a(x, y - i), at(dx=1))
        ax_m[i] = same(unit_a(x, y - i), at(dx=-1))
        b_x[i].wait_recv()
        by_p[i] = same(unit_b(x - i, y), at(dy=1))
        by_m[i] = same(unit_b(x - i, y), at(dy=-1))
    far = []
    for i in (0, 1, 3, 2):
        ax_p[i].wait_recv()
        far.append(same(unit_a(x - 1, y - i, 0, 16), at(dx=1)))
        ax_m[i].wait_recv()
        far.append(same(unit_a(x + 1, y - i, 16, 32), at(dx=-1)))
        by_p[i].wait_recv()
        far.append(same(unit_b(x - i, y - 1, 32, 48), at(dy=1)))
        by_m[i].wait_recv()
        far.append(same(unit_b(x - i, y + 1, 48, 64), at(dy=-1)))
    cap_up.wait_recv()
    relay_up = send(C.at[1024:1280], C.at[1536:1792], at(other=True))
    cap_down.wait_recv()
    relay_down = send(C.at[1280:1536], C.at[1792:2048], at(other=True))
    cap_side.wait_recv()
    relay_up.wait_recv()
    relay_down.wait_recv()
    for copy in far:
        copy.wait_recv()

    slope = temper * LOG2E
    offset = bias_value * LOG2E

    def pair_step(k, sums):
        xk, yk = (x + k) % 4, (y + k) % 4
        for i in range(4):
            V[k * 256 + i * 32 : k * 256 + i * 32 + 32, :] = G[xk, i, 0:32, :]
            V[k * 256 + 128 + i * 32 : k * 256 + 128 + i * 32 + 32, :] = G[i, yk, 32:64, :]

        def columns(j, carry):
            total, logs = carry
            cols = pl.ds(pl.multiple_of(j * 512, 512), 512)
            dots = lax.dot_general(
                V[k * 256 : k * 256 + 256, :], C[cols, :], (((1,), (1,)), ((), ())),
                preferred_element_type=F32,
            )
            grown = jnp.exp2(dots * slope + offset)
            above = 1.0 + grown
            pairs = grown * pl.reciprocal(above, approx=False)
            PR[k * 256 : k * 256 + 256, cols] = pairs.astype(BF16)
            total = total + jnp.sum(pairs.reshape(32, 8, 512), axis=0)
            quads = above.reshape(8, 4, 8, 512)
            quads = (quads[:, 0] * quads[:, 1]) * (quads[:, 2] * quads[:, 3])
            logs = logs + jnp.sum(jnp.log(quads), axis=0)
            return total, logs

        return lax.fori_loop(0, 4, columns, sums)

    def own_pairs(sums):
        total, logs = sums
        dots = lax.dot_general(
            G[x, y, own_rows, :], C[0:512, :], (((1,), (1,)), ((), ())), preferred_element_type=F32
        )
        grown = jnp.exp2(dots * slope + offset)
        part = pl.reciprocal(1.0 + grown, approx=False)
        first = (outer * 64 + inner) * OWN
        ids = first + lax.broadcasted_iota(jnp.int32, (OWN, CAP), 0)
        match = owner[...] == ids
        pairs = jnp.where(match, -part, grown * part)
        row = jnp.where(zh < 2, y * 32 + zh * 16, 128 + x * 32 + (zh - 2) * 16)
        PR[pl.ds(pl.multiple_of(row, 16), 16), 0:512] = pairs.astype(BF16)
        logits = dots * temper + bias_value
        ones = jnp.where(match, 1.0, 0.0)
        taken = jnp.where(match, logits, 0.0)
        total = total - (ones[0:8] + ones[8:16])
        logs = logs - (taken[0:8] + taken[8:16])
        return total, logs

    def video_step(k, keep, power):
        def columns(j, carry):
            cols = pl.ds(pl.multiple_of(j * 256, 256), 256)
            part = jnp.dot(
                PR[k * 256 : k * 256 + 256, :], C[:, cols], preferred_element_type=F32
            )
            with_video = part * V[k * 256 : k * 256 + 256, cols].astype(F32)
            carry = carry + jnp.sum(with_video.reshape(32, 8, 256), axis=0)
            for i in range(4):
                piece_a = part[i * 32 : i * 32 + 32]
                piece_b = part[128 + i * 32 : 128 + i * 32 + 32]
                if keep:
                    FA[i, :, cols] = piece_a
                    FB[i, :, cols] = piece_b
                else:
                    VA[k - 1, i, :, cols] = piece_a.astype(BF16)
                    VB[k - 1, i, :, cols] = piece_b.astype(BF16)
            return carry

        return lax.fori_loop(0, 4, columns, power)

    sums = (jnp.zeros((8, 512), F32), jnp.zeros((8, 512), F32))
    power = jnp.zeros((8, 256), F32)

    sums = pair_step(2, sums)
    power = video_step(2, False, power)
    first_hop = [
        send(VA.at[1, :, 0:16], R1.at[0], at(dx=1)),
        send(VB.at[1, :, 0:16], R1.at[2], at(dy=1)),
        send(VA.at[1, :, 16:32], R1.at[1], at(dx=-1)),
        send(VB.at[1, :, 16:32], R1.at[3], at(dy=-1)),
    ]
    sums = pair_step(1, sums)
    power = video_step(1, False, power)
    plain = [
        send(VA.at[0, :, 16:32], RU.at[0], at(dx=1)),
        send(VB.at[0, :, 16:32], RU.at[2], at(dy=1)),
    ]
    sums = pair_step(3, sums)
    power = video_step(3, False, power)
    plain += [
        send(VA.at[2, :, 0:16], RU.at[1], at(dx=-1)),
        send(VB.at[2, :, 0:16], RU.at[3], at(dy=-1)),
    ]
    merged = []
    for n, (ref, k, lo, device) in enumerate(
        (
            (VA, 0, 0, at(dx=1)),
            (VA, 2, 16, at(dx=-1)),
            (VB, 0, 0, at(dy=1)),
            (VB, 2, 16, at(dy=-1)),
        )
    ):
        first_hop[(0, 2, 1, 3)[n]].wait_recv()
        for i in range(4):
            TM[n, i] = (ref[k, i, lo : lo + 16, :].astype(F32) + R1[n, i].astype(F32)).astype(BF16)
        merged.append(send(TM.at[n], RM.at[n], device))
    sums = pair_step(0, sums)
    sums = own_pairs(sums)
    power = video_step(0, True, power)

    row_of = lax.broadcasted_iota(jnp.int32, (8, 128), 0)
    SC[0] = jnp.where(
        row_of == 0,
        jnp.sum(sums[1]),
        jnp.where(row_of == 1, jnp.sum(power), jnp.sum(sums[0])),
    )

    def scalar_send(stage, first_slot, devices):
        return [
            send(SC.at[stage], SC.at[first_slot + n], device) for n, device in enumerate(devices)
        ]

    def scalar_take(stage, first_slot, copies):
        value = SC[stage]
        for n, copy in enumerate(copies):
            copy.wait_recv()
            value = value + SC[first_slot + n]
        SC[stage + 1] = value

    sc_x = scalar_send(0, 8, [at(dx=i) for i in (1, 2, 3)])

    def caption_part(first):
        return lax.dot_general(
            PR[:, first : first + 256], V[...], (((0,), (0,)), ((), ())),
            preferred_element_type=F32,
        )

    for i in range(2):
        TN1[i * 256 : i * 256 + 256, :] = caption_part(1536 + i * 256).astype(BF16)
    side_near = send(TN1, RN1, at(other=True))

    for copy in plain + merged:
        copy.wait_recv()
    for i in range(4):
        for ref, n in ((FA, 0), (FB, 2)):
            low = ref[i, 0:16, :] + RM[n, i].astype(F32) + RU[n + 1, i].astype(F32)
            high = ref[i, 16:32, :] + RU[n, i].astype(F32) + RM[n + 1, i].astype(F32)
            ref[i, 0:16, :] = low
            ref[i, 16:32, :] = high
            TP[n // 2, i, 0:16, :] = low.astype(BF16)
            TP[n // 2, i, 16:32, :] = high.astype(BF16)
    second_a, second_b = [], []
    for i in (1, 3, 2):
        second_a.append(send(TP.at[0, (y + i) % 4], RP.at[0, i - 1], at(dy=i)))
        second_b.append(send(TP.at[1, (x + i) % 4], RP.at[1, i - 1], at(dx=i)))
    scalar_take(0, 8, sc_x)
    sc_y = scalar_send(1, 11, [at(dy=i) for i in (1, 2, 3)])

    near = [caption_part(1024 + i * 256) for i in range(2)]
    side_near.wait_recv()
    for i in range(2):
        rows = slice(i * 256, i * 256 + 256)
        TN2[rows, :] = (near[i] + RN1[rows, :].astype(F32)).astype(BF16)
    back_down = send(TN2.at[0:256], RN2.at[0:256], at(dz=-1))
    back_up = send(TN2.at[256:512], RN2.at[256:512], at(dz=1))

    for copy in second_a + second_b:
        copy.wait_recv()
    sum_a = FA[y] + RP[0, 0].astype(F32) + RP[0, 1].astype(F32) + RP[0, 2].astype(F32)
    sum_b = FB[x] + RP[1, 0].astype(F32) + RP[1, 1].astype(F32) + RP[1, 2].astype(F32)
    for i, value in enumerate((sum_a[0:16], sum_a[16:32], sum_b[0:16], sum_b[16:32])):
        S2[i] = value
        TZ[i] = value.astype(BF16)
    third = [send(TZ.at[(zh + i) % 4], RZ.at[i - 1], at(dz=2 * i)) for i in (1, 2, 3)]
    scalar_take(1, 11, sc_y)
    sc_z = scalar_send(2, 14, [at(dz=2 * i) for i in (1, 2, 3)])

    for i in range(2):
        TS[i * 256 : i * 256 + 256, :] = caption_part(512 + i * 256).astype(BF16)
    side = send(TS, RS, at(other=True))
    scalar_take(2, 14, sc_z)
    sc_p = scalar_send(3, 17, [device_at(x, y, zh * 2 + 1 - zp, core)])
    for i in range(2):
        CG[i * 256 : i * 256 + 256, :] = caption_part(i * 256)
    scalar_take(3, 17, sc_p)
    sc_c = scalar_send(4, 18, [at(other=True)])

    for copy in third:
        copy.wait_recv()
    wide = videos[...].astype(F32)
    video_scale = lax.rsqrt(jnp.sum(wide * wide, axis=1, keepdims=True) + 1e-06)
    unit = wide * video_scale
    grad = temper * (
        S2[zh] + RZ[0].astype(F32) + RZ[1].astype(F32) + RZ[2].astype(F32)
    )
    video_out[...] = video_scale * (grad - unit * jnp.sum(unit * grad, axis=1, keepdims=True))

    scalar_take(4, 18, sc_c)
    scale_of = jnp.where(row_of == 1, jnp.broadcast_to(temper, (8, 128)), 1.0)
    scalar_out[...] = SC[5] * scale_of * (1.0 / 536870912.0)

    side.wait_recv()
    back_down.wait_recv()
    back_up.wait_recv()

    def finish(i, carry):
        rows = pl.ds(pl.multiple_of(i * 64, 64), 64)
        block = captions[rows, :].astype(F32)
        scale = lax.rsqrt(jnp.sum(block * block, axis=1, keepdims=True) + 1e-06)
        unit = block * scale
        grad = temper * (CG[rows, :] + RS[rows, :].astype(F32) + RN2[rows, :].astype(F32))
        caption_out[rows, :] = scale * (grad - unit * jnp.sum(unit * grad, axis=1, keepdims=True))
        return carry

    lax.fori_loop(0, CAP // 64, finish, 0)
    for copy in started:
        copy.wait_send()


def on_device(videos, captions, caption_owner, log_temp, bias):
    vmem = pl.BlockSpec(memory_space=pltpu.VMEM)
    smem = pl.BlockSpec(memory_space=pltpu.SMEM)
    V = pltpu.VMEM
    video_grad, caption_grad, scalars = pl.pallas_call(
        kernel,
        out_shape=(
            jax.ShapeDtypeStruct((OWN, D), F32),
            jax.ShapeDtypeStruct((CAP, D), F32),
            jax.ShapeDtypeStruct((8, 128), F32),
        ),
        in_specs=[vmem, vmem, vmem, smem, smem],
        out_specs=(vmem, vmem, vmem),
        scratch_shapes=[
            V((4, 4, 64, D), BF16),
            V((ALL, D), BF16),
            V((1024, D), BF16),
            V((1024, ALL), BF16),
            V((3, 4, 32, D), BF16),
            V((3, 4, 32, D), BF16),
            V((4, 32, D), F32),
            V((4, 32, D), F32),
            V((4, 4, 16, D), BF16),
            V((4, 4, 16, D), BF16),
            V((4, 4, 16, D), BF16),
            V((4, 4, 16, D), BF16),
            V((2, 4, 32, D), BF16),
            V((2, 3, 32, D), BF16),
            V((4, OWN, D), F32),
            V((4, OWN, D), BF16),
            V((3, OWN, D), BF16),
            V((CAP, D), BF16),
            V((CAP, D), BF16),
            V((CAP, D), BF16),
            V((CAP, D), BF16),
            V((CAP, D), BF16),
            V((CAP, D), BF16),
            V((CAP, D), F32),
            V((19, 8, 128), F32),
            pltpu.SemaphoreType.DMA((COPIES,)),
            pltpu.SemaphoreType.DMA((COPIES,)),
        ],
        compiler_params=pltpu.CompilerParams(
            collective_id=0, has_side_effects=True, vmem_limit_bytes=56 * 2**20
        ),
        cost_estimate=pl.CostEstimate(
            flops=3 * 2 * 1024 * ALL * D, bytes_accessed=4 * 2**20, transcendentals=3 * 1024 * ALL
        ),
    )(videos, captions, caption_owner.reshape(1, CAP), log_temp, bias)
    return video_grad, caption_grad, scalars[:3, 0]


def solution(mesh):
    in_specs = (P(("outer", "dp"), None), P(("outer", "dp"), None), P(("outer", "dp")), P(), P())
    out_specs = (P(("outer", "dp"), None), P(("outer", "dp"), None), P())
    return jax.shard_map(
        on_device, mesh=mesh, in_specs=in_specs, out_specs=out_specs, check_vma=False
    )
```

time: 1620 us -> 89.3 us (0.06)
  waiting for transfers between devices: 1330 us -> 0 us
  starting transfers between devices: 108 us -> 0 us
  Pallas kernels: 0 us -> 81.2 us
  blocking collectives: 76.5 us -> 0 us
  matrix products: 57.1 us -> 0 us
    reduce_scatter x4 -> x0, waiting for transfers between devices: 985 us -> none  [on_device(): lax.psum_scatter(video_part, 'dp', scatter_dimension=0, tiled=True)]
    all_gather x1 -> x0, waiting for transfers between devices: 258 us -> none  [on_device(): panel_low = lax.all_gather(video_low, 'dp', axis=0, tiled=True)]
    ppermute x3 -> x0, waiting for transfers between devices: 83.1 us -> none  [from_behind(): return lax.ppermute(value, axis, pairs)]
    pallas_call x0 -> x1, Pallas kernels: none -> 81.2 us  [on_device(): pl.pallas_call(kernel, out_shape=(jax.ShapeDtypeStruct((OWN, D), F32), ja...]
    psum x1 -> x0, blocking collectives: 76.5 us -> none  [on_device(): totals = lax.psum(totals, ('outer', 'dp'))]
    dot_general x12 -> x0, matrix products: 57.1 us -> none  [the longest x4 22.1 us: pair_block(): lax.dot_general(video_rows, caption_low, (((1,), (1,)), ((), ())), prefer...]
    ppermute x3 -> x0, starting transfers between devices: 55.3 us -> none  [from_behind(): return lax.ppermute(value, axis, pairs)]
    all_to_all x1 -> x0, starting transfers between devices: 52.8 us -> none  [on_device(): lax.all_to_all(return_slots, 'outer', split_axis=0, concat_axis=0, tiled=...]
  transfers between devices with their start and end apart: 9 -> 0, of which waited for: 9 -> 0; matrix products, arithmetic and copies ran while one was open for 4% -> 0% of each run, Pallas kernels for 0% -> 0%
where the time goes in v1:
time: 89.3 us; the launch traced here: 89 us
  Pallas kernels  81.2 us (91%)
  local copies, waits for them, and re-layouts  5.94 us (7%)
  between operations  1.93 us (2%)
    pallas_call x1, Pallas kernels, on_device(): pl.pallas_call(kernel, out_shape=(jax.ShapeDtypeStruct((OWN, D), F32), ja...  81.2 us
    unnamed x2, local copies, waits for them, and re-layouts  4.63 us

profile of v1, /device:TPU:1, one launch (start us, length us, event | category | flops | bytes accessed | tf_op | source)
XLA Modules:
  0.0 89.0 jit_solution(9380216390387735070)
XLA Ops:
  1.9 81.2 %shard_map.76 = (f32[16,1024]{1,0:T(8,128)}, f32[512,1024]{1,0:T(8,128)}, f32[8,128]{1,0:T(8,128)}) custom-call(bf16[16,1024]{1,0:T(8,128)(2,1)} %videos.1, bf16[512,1024]{1,0:T(8,128)(2,1)} %captions.1, s32[1,512]{1,0:T(1,128)} %bitcast.1, f32[1]{0:T(128)S(6)} %copy.10.log_temp, f32[1]{0:T(128)S(6)} %copy.11.bias), custom_call_target="tpu_custom_call" | custom-call | flops 12884901888 | bytes 4194304 | tf_op jit(solution)/shard_map/pallas_call | solution.py:356
  83.1 1.3 %slice_reduce_fusion = f32[3]{0:T(128)} fusion(f32[8,128]{1,0:T(8,128)} %get-tuple-element.8), kind=kLoop, calls=%fused_computation | loop fusion | bytes 24 | tf_op jit(solution)/shard_map/slice | solution.py:401
  84.4 1.5 %copy.12 = f32[16,1024]{1,0:T(8,128)} copy(f32[16,1024]{1,0:T(8,128)} %get-tuple-element.12) | data formatting | bytes 131072
  85.9 3.2 %copy.13 = f32[512,1024]{1,0:T(8,128)} copy(f32[512,1024]{1,0:T(8,128)} %get-tuple-element.13) | data formatting | bytes 4194304

commit v2 on v1

v2 whole, which is shorter than its diff:
```python
import jax
import jax.numpy as jnp
from jax import lax
from jax.experimental import pallas as pl
from jax.experimental.pallas import tpu as pltpu
from jax.sharding import PartitionSpec as P

MESH = pl.DeviceIdType.MESH
F32 = jnp.float32
BF16 = jnp.bfloat16
LOG2E = 1.4426950408889634
D = 1024
OWN = 16
CAP = 512
ALL = 4 * CAP
COPIES = 96


def device_at(x, y, z, core):
    return ((x // 2) * 2 + core, (y * 2 + x % 2) * 8 + z)


def kernel(
    videos_far, captions_far, owner_far, log_temp, bias,
    video_out, caption_out, scalar_out,
    G, C, V, PR, VA, VB, FA, FB,
    RA, RB, TP, RP, S2, TZ, RZ,
    TN1, RN1, TN2, RN2, TS, RS, CG, SC,
    videos, captions, owner, send_sem, recv_sem, local_sem,
):
    outer, inner = lax.axis_index("outer"), lax.axis_index("dp")
    x = (outer // 2) * 2 + (inner // 8) % 2
    y = inner // 16
    z = inner % 8
    core = outer % 2
    zh, zp = z // 2, z % 2

    def at(dx=0, dy=0, dz=0, other=False):
        return device_at(
            (x + dx + 4) % 4, (y + dy + 4) % 4, (z + dz + 8) % 8, 1 - core if other else core
        )

    started = []

    def send(src, dst, device):
        index = len(started)
        copy = pltpu.make_async_remote_copy(
            src_ref=src, dst_ref=dst, send_sem=send_sem.at[index], recv_sem=recv_sem.at[index],
            device_id=device, device_id_type=MESH,
        )
        copy.start()
        started.append(copy)
        return copy

    partners = [at(dx=i) for i in (1, 2, 3)] + [at(dy=i) for i in (1, 2, 3)]
    partners += [at(dz=i) for i in (1, 2, 4, 6, 7)] + [at(other=True)]
    barrier = pltpu.get_barrier_semaphore()
    for device in partners:
        pl.semaphore_signal(barrier, inc=1, device_id=device, device_id_type=MESH)

    bring_videos = pltpu.make_async_copy(videos_far, videos, local_sem.at[8])
    bring_videos.start()
    bring = []
    for i in range(4):
        rows = pl.ds(i * 128, 128)
        bring.append(
            pltpu.make_async_copy(captions_far.at[rows], captions.at[rows], local_sem.at[i])
        )
    bring.append(pltpu.make_async_copy(owner_far, owner, local_sem.at[7]))
    for copy in bring:
        copy.start()
    temper = jnp.exp(jnp.full((1, 1), log_temp[0], F32))
    bias_value = bias[0]

    bring_videos.wait()
    wide = videos[...].astype(F32)
    video_scale = lax.rsqrt(jnp.sum(wide * wide, axis=1, keepdims=True) + 1e-06)
    own_rows = pl.ds(pl.multiple_of(zh * OWN, OWN), OWN)
    G[x, y, own_rows, :] = (wide * video_scale).astype(BF16)

    pl.semaphore_wait(barrier, len(partners))

    mine = G.at[x, y, own_rows]
    along_z = [send(mine, mine, at(dz=2 * i)) for i in (1, 2, 3)]
    def low_captions(i, carry):
        rows = pl.ds(pl.multiple_of(i * 128, 128), 128)
        block = captions[rows, :].astype(F32)
        scale = lax.rsqrt(jnp.sum(block * block, axis=1, keepdims=True) + 1e-06)
        C[rows, :] = (block * scale).astype(BF16)
        return carry

    for copy in bring:
        copy.wait()
    lax.fori_loop(0, CAP // 128, low_captions, 0)
    cap_up = send(C.at[0:256], C.at[1024:1280], at(dz=1))
    cap_down = send(C.at[256:512], C.at[1280:1536], at(dz=-1))
    cap_side = send(C.at[0:512], C.at[512:1024], at(other=True))
    for copy in along_z:
        copy.wait_recv()

    def unit_a(px, py, lo=0, hi=32):
        return G.at[(px + 4) % 4, (py + 4) % 4, lo:hi]

    def unit_b(px, py, lo=32, hi=64):
        return G.at[(px + 4) % 4, (py + 4) % 4, lo:hi]

    def same(unit, device):
        return send(unit, unit, device)

    ax_p, ax_m, by_p, by_m = {}, {}, {}, {}
    a_y, b_x = {}, {}
    for i in (2, 1, 3):
        a_y[i] = same(unit_a(x, y), at(dy=i))
        b_x[i] = same(unit_b(x, y), at(dx=i))
    ax_p[0] = same(unit_a(x, y), at(dx=1))
    by_p[0] = same(unit_b(x, y), at(dy=1))
    ax_m[0] = same(unit_a(x, y), at(dx=-1))
    by_m[0] = same(unit_b(x, y), at(dy=-1))
    for i in (1, 3, 2):
        a_y[i].wait_recv()
        ax_p[i] = same(unit_a(x, y - i), at(dx=1))
        ax_m[i] = same(unit_a(x, y - i), at(dx=-1))
        b_x[i].wait_recv()
        by_p[i] = same(unit_b(x - i, y), at(dy=1))
        by_m[i] = same(unit_b(x - i, y), at(dy=-1))
    far = []

    def pass_on(i):
        ax_p[i].wait_recv()
        far.append(same(unit_a(x - 1, y - i, 0, 16), at(dx=1)))
        ax_m[i].wait_recv()
        far.append(same(unit_a(x + 1, y - i, 16, 32), at(dx=-1)))
        by_p[i].wait_recv()
        far.append(same(unit_b(x - i, y - 1, 32, 48), at(dy=1)))
        by_m[i].wait_recv()
        far.append(same(unit_b(x - i, y + 1, 48, 64), at(dy=-1)))

    slope = temper * LOG2E
    offset = bias_value * LOG2E

    def collect(k):
        xk, yk = (x + k) % 4, (y + k) % 4
        for i in range(4):
            V[k * 256 + i * 32 : k * 256 + i * 32 + 32, :] = G[xk, i, 0:32, :]
            V[k * 256 + 128 + i * 32 : k * 256 + 128 + i * 32 + 32, :] = G[i, yk, 32:64, :]

    def pair_step(k, half, sums):
        total, logs, power = sums
        rows = slice(k * 256, k * 256 + 256)
        cols = slice(half * 1024, half * 1024 + 1024)
        dots = lax.dot_general(
            V[rows, :], C[cols, :], (((1,), (1,)), ((), ())), preferred_element_type=F32
        )
        grown = jnp.exp2(dots * slope + offset)
        above = 1.0 + grown
        pairs = grown * pl.reciprocal(above, approx=False)
        PR[rows, cols] = pairs.astype(BF16)
        total = total + jnp.sum(pairs.reshape(32, 8, 1024), axis=0)
        quads = above.reshape(8, 4, 8, 1024)
        quads = (quads[:, 0] * quads[:, 1]) * (quads[:, 2] * quads[:, 3])
        logs = logs + jnp.sum(jnp.log(quads), axis=0)
        power = power + jnp.sum((pairs * dots).reshape(32, 8, 1024), axis=0)
        return total, logs, power

    def own_pairs():
        dots = lax.dot_general(
            G[x, y, own_rows, :], C[0:512, :], (((1,), (1,)), ((), ())), preferred_element_type=F32
        )
        grown = jnp.exp2(dots * slope + offset)
        part = pl.reciprocal(1.0 + grown, approx=False)
        first = (outer * 64 + inner) * OWN
        ids = first + lax.broadcasted_iota(jnp.int32, (OWN, CAP), 0)
        match = owner[...] == ids
        pairs = jnp.where(match, -part, grown * part)
        row = jnp.where(zh < 2, y * 32 + zh * 16, 128 + x * 32 + (zh - 2) * 16)
        PR[pl.ds(pl.multiple_of(row, 16), 16), 0:512] = pairs.astype(BF16)
        logits = dots * temper + bias_value
        ones = jnp.where(match, 1.0, 0.0)
        taken = jnp.where(match, logits, 0.0)
        SC[20] = jnp.full((8, 128), jnp.sum(ones), F32)
        SC[21] = jnp.full((8, 128), jnp.sum(taken), F32)
        SC[22] = jnp.full((8, 128), jnp.sum(jnp.where(match, dots, 0.0)), F32)

    def video_step(k):
        part = jnp.dot(PR[k * 256 : k * 256 + 256, :], C[...], preferred_element_type=F32)
        for i in range(4):
            piece_a = part[i * 32 : i * 32 + 32]
            piece_b = part[128 + i * 32 : 128 + i * 32 + 32]
            if k == 0:
                FA[i] = piece_a
                FB[i] = piece_b
            else:
                VA[k - 1, i] = piece_a.astype(BF16)
                VB[k - 1, i] = piece_b.astype(BF16)

    def video_send(k):
        return [
            send(VA.at[k - 1], RA.at[k - 1], at(dx=k)),
            send(VB.at[k - 1], RB.at[k - 1], at(dy=k)),
        ]

    def caption_part(first):
        return lax.dot_general(
            PR[:, first : first + 512], V[...], (((0,), (0,)), ((), ())),
            preferred_element_type=F32,
        )

    sums = (jnp.zeros((8, 1024), F32),) * 3

    pass_on(0)
    cap_side.wait_recv()
    collect(0)
    sums = pair_step(0, 0, sums)
    own_pairs()
    for i in (1, 3, 2):
        pass_on(i)
    for k in (1, 3):
        collect(k)
        sums = pair_step(k, 0, sums)
    cap_up.wait_recv()
    relay_up = send(C.at[1024:1280], C.at[1536:1792], at(other=True))
    cap_down.wait_recv()
    relay_down = send(C.at[1280:1536], C.at[1792:2048], at(other=True))
    relay_up.wait_recv()
    relay_down.wait_recv()
    first = []
    for k in (1, 3):
        sums = pair_step(k, 1, sums)
        video_step(k)
        first += video_send(k)
    for copy in far:
        copy.wait_recv()
    collect(2)
    for half in (0, 1):
        sums = pair_step(2, half, sums)
    video_step(2)
    first += video_send(2)
    sums = pair_step(0, 1, sums)

    row_of = lax.broadcasted_iota(jnp.int32, (8, 128), 0)
    SC[0] = jnp.where(
        row_of == 0,
        jnp.sum(sums[1]) - SC[21],
        jnp.where(row_of == 1, jnp.sum(sums[2]) - SC[22], jnp.sum(sums[0]) - SC[20]),
    )

    def scalar_send(stage, first_slot, devices):
        return [
            send(SC.at[stage], SC.at[first_slot + n], device) for n, device in enumerate(devices)
        ]

    def scalar_take(stage, first_slot, copies):
        value = SC[stage]
        for n, copy in enumerate(copies):
            copy.wait_recv()
            value = value + SC[first_slot + n]
        SC[stage + 1] = value

    sc_x = scalar_send(0, 8, [at(dx=i) for i in (1, 2, 3)])

    TN1[...] = caption_part(1536).astype(BF16)
    side_near = send(TN1, RN1, at(other=True))
    near = caption_part(1024)
    side_near.wait_recv()
    TN2[...] = (near + RN1[...].astype(F32)).astype(BF16)
    back_down = send(TN2.at[0:256], RN2.at[0:256], at(dz=-1))
    back_up = send(TN2.at[256:512], RN2.at[256:512], at(dz=1))
    scalar_take(0, 8, sc_x)
    sc_y = scalar_send(1, 11, [at(dy=i) for i in (1, 2, 3)])
    video_step(0)

    for copy in first:
        copy.wait_recv()
    for i in range(4):
        for n, (ref, more) in enumerate(((FA, RA), (FB, RB))):
            value = ref[i] + more[0, i].astype(F32) + more[1, i].astype(F32) + more[2, i].astype(F32)
            ref[i] = value
            TP[n, i] = value.astype(BF16)
    second_a, second_b = [], []
    for i in (1, 3, 2):
        second_a.append(send(TP.at[0, (y + i) % 4], RP.at[0, i - 1], at(dy=i)))
        second_b.append(send(TP.at[1, (x + i) % 4], RP.at[1, i - 1], at(dx=i)))
    scalar_take(1, 11, sc_y)
    sc_z = scalar_send(2, 14, [at(dz=2 * i) for i in (1, 2, 3)])
    TS[...] = caption_part(512).astype(BF16)
    side = send(TS, RS, at(other=True))

    for copy in second_a + second_b:
        copy.wait_recv()
    sum_a = FA[y] + RP[0, 0].astype(F32) + RP[0, 1].astype(F32) + RP[0, 2].astype(F32)
    sum_b = FB[x] + RP[1, 0].astype(F32) + RP[1, 1].astype(F32) + RP[1, 2].astype(F32)
    for i, value in enumerate((sum_a[0:16], sum_a[16:32], sum_b[0:16], sum_b[16:32])):
        S2[i] = value
        TZ[i] = value.astype(BF16)
    third = [send(TZ.at[(zh + i) % 4], RZ.at[i - 1], at(dz=2 * i)) for i in (1, 2, 3)]
    scalar_take(2, 14, sc_z)
    sc_p = scalar_send(3, 17, [device_at(x, y, zh * 2 + 1 - zp, core)])
    CG[...] = caption_part(0)
    scalar_take(3, 17, sc_p)
    sc_c = scalar_send(4, 18, [at(other=True)])

    for copy in third:
        copy.wait_recv()
    wide = videos[...].astype(F32)
    video_scale = lax.rsqrt(jnp.sum(wide * wide, axis=1, keepdims=True) + 1e-06)
    unit = wide * video_scale
    grad = temper * (
        S2[zh] + RZ[0].astype(F32) + RZ[1].astype(F32) + RZ[2].astype(F32)
    )
    video_out[...] = video_scale * (grad - unit * jnp.sum(unit * grad, axis=1, keepdims=True))

    scalar_take(4, 18, sc_c)
    scale_of = jnp.where(row_of == 1, jnp.broadcast_to(temper, (8, 128)), 1.0)
    scalar_out[...] = SC[5] * scale_of * (1.0 / 536870912.0)

    side.wait_recv()
    back_down.wait_recv()
    back_up.wait_recv()

    def finish(i, carry):
        rows = pl.ds(pl.multiple_of(i * 64, 64), 64)
        block = captions[rows, :].astype(F32)
        scale = lax.rsqrt(jnp.sum(block * block, axis=1, keepdims=True) + 1e-06)
        unit = block * scale
        grad = temper * (CG[rows, :] + RS[rows, :].astype(F32) + RN2[rows, :].astype(F32))
        caption_out[rows, :] = scale * (grad - unit * jnp.sum(unit * grad, axis=1, keepdims=True))
        return carry

    lax.fori_loop(0, CAP // 64, finish, 0)
    for copy in started:
        copy.wait_send()


def hand_out(video_grad, caption_grad, scalars, video_out, caption_out, scalar_out, sem):
    copies = [pltpu.make_async_copy(video_grad, video_out, sem.at[8])]
    for i in range(8):
        rows = pl.ds(i * (CAP // 8), CAP // 8)
        copies.append(
            pltpu.make_async_copy(caption_grad.at[rows], caption_out.at[rows], sem.at[i])
        )
    for copy in copies:
        copy.start()
    for i in range(3):
        scalar_out[i] = scalars[i, 0]
    for copy in copies:
        copy.wait()


def on_device(videos, captions, caption_owner, log_temp, bias):
    vmem = pl.BlockSpec(memory_space=pltpu.VMEM)
    smem = pl.BlockSpec(memory_space=pltpu.SMEM)
    hbm = pl.BlockSpec(memory_space=pltpu.HBM)
    V = pltpu.VMEM
    video_grad, caption_grad, scalars = pl.pallas_call(
        kernel,
        out_shape=(
            pltpu.VMEM((OWN, D), F32),
            pltpu.VMEM((CAP, D), F32),
            pltpu.VMEM((8, 128), F32),
        ),
        in_specs=[hbm, hbm, hbm, smem, smem],
        out_specs=(vmem, vmem, vmem),
        scratch_shapes=[
            V((4, 4, 64, D), BF16),
            V((ALL, D), BF16),
            V((1024, D), BF16),
            V((1024, ALL), BF16),
            V((3, 4, 32, D), BF16),
            V((3, 4, 32, D), BF16),
            V((4, 32, D), F32),
            V((4, 32, D), F32),
            V((3, 4, 32, D), BF16),
            V((3, 4, 32, D), BF16),
            V((2, 4, 32, D), BF16),
            V((2, 3, 32, D), BF16),
            V((4, OWN, D), F32),
            V((4, OWN, D), BF16),
            V((3, OWN, D), BF16),
            V((CAP, D), BF16),
            V((CAP, D), BF16),
            V((CAP, D), BF16),
            V((CAP, D), BF16),
            V((CAP, D), BF16),
            V((CAP, D), BF16),
            V((CAP, D), F32),
            V((23, 8, 128), F32),
            V((OWN, D), BF16),
            V((CAP, D), BF16),
            V((1, CAP), jnp.int32),
            pltpu.SemaphoreType.DMA((COPIES,)),
            pltpu.SemaphoreType.DMA((COPIES,)),
            pltpu.SemaphoreType.DMA((9,)),
        ],
        compiler_params=pltpu.CompilerParams(
            collective_id=0, has_side_effects=True, vmem_limit_bytes=61 * 2**20
        ),
        cost_estimate=pl.CostEstimate(
            flops=3 * 2 * 1024 * ALL * D, bytes_accessed=4 * 2**20, transcendentals=3 * 1024 * ALL
        ),
    )(
        pltpu.with_memory_space_constraint(videos, pltpu.HBM),
        pltpu.with_memory_space_constraint(captions, pltpu.HBM),
        pltpu.with_memory_space_constraint(caption_owner.reshape(1, CAP), pltpu.HBM),
        log_temp,
        bias,
    )
    video_grad, caption_grad, scalars = pl.pallas_call(
        hand_out,
        out_shape=(
            pltpu.HBM((OWN, D), F32),
            pltpu.HBM((CAP, D), F32),
            jax.ShapeDtypeStruct((3,), F32),
        ),
        in_specs=[vmem, vmem, smem],
        out_specs=(hbm, hbm, smem),
        scratch_shapes=[pltpu.SemaphoreType.DMA((9,))],
    )(video_grad, caption_grad, scalars)
    return video_grad, caption_grad, scalars


def solution(mesh):
    in_specs = (P(("outer", "dp"), None), P(("outer", "dp"), None), P(("outer", "dp")), P(), P())
    out_specs = (P(("outer", "dp"), None), P(("outer", "dp"), None), P())
    return jax.shard_map(
        on_device, mesh=mesh, in_specs=in_specs, out_specs=out_specs, check_vma=False
    )
```

time: 89.3 us -> 75.2 us (0.84)
  Pallas kernels: 81.2 us -> 70.4 us
  local copies, waits for them, and re-layouts: 5.94 us -> 2.53 us
    pallas_call x1 -> x2, Pallas kernels: 81.2 us -> 70.4 us  [the longest x1 66.9 us: on_device(): pl.pallas_call(kernel, out_shape=(pltpu.VMEM((OWN, D), F32), pltpu.VMEM((...]
    unnamed x2 -> x6, local copies, waits for them, and re-layouts: 4.63 us -> 2.53 us
    slice x1 -> x0, local copies, waits for them, and re-layouts: 1.31 us -> none  [on_device(): return (video_grad, caption_grad, scalars[:3, 0])]
where the time goes in v2:
time: 75.2 us; the launch traced here: 75 us
  Pallas kernels  70.4 us (94%)
  local copies, waits for them, and re-layouts  2.53 us (3%)
  between operations  2.1 us (3%)
    pallas_call x1, Pallas kernels, on_device(): pl.pallas_call(kernel, out_shape=(pltpu.VMEM((OWN, D), F32), pltpu.VMEM((...  66.9 us
    pallas_call x1, Pallas kernels, on_device(): pl.pallas_call(hand_out, out_shape=(pltpu.HBM((OWN, D), F32), pltpu.HBM((...  3.56 us
    unnamed x6, local copies, waits for them, and re-layouts  2.53 us

profile of v2, /device:TPU:1, one launch (start us, length us, event | category | flops | bytes accessed | tf_op | source)
XLA Modules:
  0.0 75.0 jit_solution(6151196062434817686)
XLA Ops:
  1.9 66.9 %shard_map.76 = (f32[16,1024]{1,0:T(8,128)S(1)}, f32[512,1024]{1,0:T(8,128)S(1)}, f32[8,128]{1,0:T(8,128)S(1)}) custom-call(bf16[16,1024]{1,0:T(8,128)(2,1)} %videos_far.1, bf16[512,1024]{1,0:T(8,128)(2,1)} %captions_far.1, s32[1,512]{1,0:T(1,128)} %bitcast.1, f32[1]{0:T(128)S(6)} %copy.8.log_temp, f32[1]{0:T(128)S(6)} %copy.9.bias), custom_call_target="tpu_custom_call" | custom-call | flops 12884901888 | bytes 4194304 | tf_op jit(solution)/shard_map/pallas_call | solution.py:354
  68.8 0.0 copy-start
  68.8 1.3 %copy-done = f32[512,1024]{1,0:T(8,128)} copy-done((f32[512,1024]{1,0:T(8,128)}, f32[512,1024]{1,0:T(8,128)S(1)}, u32[]{:S(2)}) %copy-start) | copy-done | bytes 2097176
  70.1 0.0 copy-start.1
  70.1 0.6 copy-done.1
  70.7 0.0 copy-start.2
  70.7 0.6 copy-done.2
  71.3 3.6 %shard_map.77 = (f32[16,1024]{1,0:T(8,128)}, f32[512,1024]{1,0:T(8,128)}, f32[3]{0:T(128)}) custom-call(f32[16,1024]{1,0:T(8,128)} %copy-done.1, f32[512,1024]{1,0:T(8,128)} %copy-done, f32[8,128]{1,0:T(8,128)} %copy-done.2), custom_call_target="tpu_custom_call" | custom-call | tf_op jit(solution)/shard_map/pallas_call | solution.py:407
Async XLA Ops:
  68.8 1.3 %copy-start = (f32[512,1024]{1,0:T(8,128)}, f32[512,1024]{1,0:T(8,128)S(1)}, u32[]{:S(2)}) copy-start(f32[512,1024]{1,0:T(8,128)S(1)} %get-tuple-element.7.caption_grad) | copy-start | bytes 6291460
  70.1 0.6 copy-start.1
  70.7 0.6 copy-start.2

commit v3 on v2

--- a/solution.py
+++ b/solution.py
@@ -256,36 +256,38 @@
             value = value + SC[first_slot + n]
         SC[stage + 1] = value
 
-    sc_x = scalar_send(0, 8, [at(dx=i) for i in (1, 2, 3)])
+    sc_z = scalar_send(0, 8, [at(dz=2 * i) for i in (1, 2, 3)])
 
     TN1[...] = caption_part(1536).astype(BF16)
     side_near = send(TN1, RN1, at(other=True))
-    near = caption_part(1024)
+    CG[...] = caption_part(1024)
+    video_step(0)
+    scalar_take(0, 8, sc_z)
+    sc_p = scalar_send(1, 11, [device_at(x, y, zh * 2 + 1 - zp, core)])
     side_near.wait_recv()
-    TN2[...] = (near + RN1[...].astype(F32)).astype(BF16)
+    TN2[...] = (CG[...] + RN1[...].astype(F32)).astype(BF16)
     back_down = send(TN2.at[0:256], RN2.at[0:256], at(dz=-1))
     back_up = send(TN2.at[256:512], RN2.at[256:512], at(dz=1))
-    scalar_take(0, 8, sc_x)
-    sc_y = scalar_send(1, 11, [at(dy=i) for i in (1, 2, 3)])
-    video_step(0)
-
-    for copy in first:
-        copy.wait_recv()
-    for i in range(4):
-        for n, (ref, more) in enumerate(((FA, RA), (FB, RB))):
+
+    second = []
+    for n, (ref, more) in enumerate(((FA, RA), (FB, RB))):
+        for copy in first[n::2]:
+            copy.wait_recv()
+        for i in range(4):
             value = ref[i] + more[0, i].astype(F32) + more[1, i].astype(F32) + more[2, i].astype(F32)
             ref[i] = value
             TP[n, i] = value.astype(BF16)
-    second_a, second_b = [], []
-    for i in (1, 3, 2):
-        second_a.append(send(TP.at[0, (y + i) % 4], RP.at[0, i - 1], at(dy=i)))
-        second_b.append(send(TP.at[1, (x + i) % 4], RP.at[1, i - 1], at(dx=i)))
-    scalar_take(1, 11, sc_y)
-    sc_z = scalar_send(2, 14, [at(dz=2 * i) for i in (1, 2, 3)])
+        for i in (2, 1, 3):
+            if n == 0:
+                second.append(send(TP.at[0, (y + i) % 4], RP.at[0, i - 1], at(dy=i)))
+            else:
+                second.append(send(TP.at[1, (x + i) % 4], RP.at[1, i - 1], at(dx=i)))
+    scalar_take(1, 11, sc_p)
+    sc_c = scalar_send(2, 12, [at(other=True)])
     TS[...] = caption_part(512).astype(BF16)
     side = send(TS, RS, at(other=True))
 
-    for copy in second_a + second_b:
+    for copy in second:
         copy.wait_recv()
     sum_a = FA[y] + RP[0, 0].astype(F32) + RP[0, 1].astype(F32) + RP[0, 2].astype(F32)
     sum_b = FB[x] + RP[1, 0].astype(F32) + RP[1, 1].astype(F32) + RP[1, 2].astype(F32)
@@ -293,11 +295,11 @@
         S2[i] = value
         TZ[i] = value.astype(BF16)
     third = [send(TZ.at[(zh + i) % 4], RZ.at[i - 1], at(dz=2 * i)) for i in (1, 2, 3)]
-    scalar_take(2, 14, sc_z)
-    sc_p = scalar_send(3, 17, [device_at(x, y, zh * 2 + 1 - zp, core)])
+    scalar_take(2, 12, sc_c)
+    sc_x = scalar_send(3, 13, [at(dx=i) for i in (1, 2, 3)])
     CG[...] = caption_part(0)
-    scalar_take(3, 17, sc_p)
-    sc_c = scalar_send(4, 18, [at(other=True)])
+    scalar_take(3, 13, sc_x)
+    sc_y = scalar_send(4, 16, [at(dy=i) for i in (1, 2, 3)])
 
     for copy in third:
         copy.wait_recv()
@@ -309,7 +311,7 @@
     )
     video_out[...] = video_scale * (grad - unit * jnp.sum(unit * grad, axis=1, keepdims=True))
 
-    scalar_take(4, 18, sc_c)
+    scalar_take(4, 16, sc_y)
     scale_of = jnp.where(row_of == 1, jnp.broadcast_to(temper, (8, 128)), 1.0)
     scalar_out[...] = SC[5] * scale_of * (1.0 / 536870912.0)
 

time: 75.2 us -> 74.8 us (level)
  no operation moved by 1% of the time
where the time goes in v3:
time: 74.8 us; the launch traced here: 74.6 us
  Pallas kernels  70 us (94%)
  local copies, waits for them, and re-layouts  2.53 us (3%)
  between operations  2.1 us (3%)
    pallas_call x1, Pallas kernels, on_device(): pl.pallas_call(kernel, out_shape=(pltpu.VMEM((OWN, D), F32), pltpu.VMEM((...  66.4 us
    pallas_call x1, Pallas kernels, on_device(): pl.pallas_call(hand_out, out_shape=(pltpu.HBM((OWN, D), F32), pltpu.HBM((...  3.56 us
    unnamed x6, local copies, waits for them, and re-layouts  2.53 us

profile of v3, /device:TPU:1, one launch (start us, length us, event | category | flops | bytes accessed | tf_op | source)
XLA Modules:
  0.0 74.6 jit_solution(8616166943748697437)
XLA Ops:
  1.9 66.4 %shard_map.76 = (f32[16,1024]{1,0:T(8,128)S(1)}, f32[512,1024]{1,0:T(8,128)S(1)}, f32[8,128]{1,0:T(8,128)S(1)}) custom-call(bf16[16,1024]{1,0:T(8,128)(2,1)} %videos_far.1, bf16[512,1024]{1,0:T(8,128)(2,1)} %captions_far.1, s32[1,512]{1,0:T(1,128)} %bitcast.1, f32[1]{0:T(128)S(6)} %copy.8.log_temp, f32[1]{0:T(128)S(6)} %copy.9.bias), custom_call_target="tpu_custom_call" | custom-call | flops 12884901888 | bytes 4194304 | tf_op jit(solution)/shard_map/pallas_call | solution.py:356
  68.4 0.0 copy-start
  68.4 1.3 %copy-done = f32[512,1024]{1,0:T(8,128)} copy-done((f32[512,1024]{1,0:T(8,128)}, f32[512,1024]{1,0:T(8,128)S(1)}, u32[]{:S(2)}) %copy-start) | copy-done | bytes 2097176
  69.7 0.0 copy-start.1
  69.7 0.6 copy-done.1
  70.3 0.0 copy-start.2
  70.3 0.6 copy-done.2
  70.9 3.6 %shard_map.77 = (f32[16,1024]{1,0:T(8,128)}, f32[512,1024]{1,0:T(8,128)}, f32[3]{0:T(128)}) custom-call(f32[16,1024]{1,0:T(8,128)} %copy-done.1, f32[512,1024]{1,0:T(8,128)} %copy-done, f32[8,128]{1,0:T(8,128)} %copy-done.2), custom_call_target="tpu_custom_call" | custom-call | tf_op jit(solution)/shard_map/pallas_call | solution.py:409
Async XLA Ops:
  68.4 1.3 %copy-start = (f32[512,1024]{1,0:T(8,128)}, f32[512,1024]{1,0:T(8,128)S(1)}, u32[]{:S(2)}) copy-start(f32[512,1024]{1,0:T(8,128)S(1)} %get-tuple-element.7.caption_grad) | copy-start | bytes 6291460
  69.7 0.6 copy-start.1
  70.3 0.6 copy-start.2
